TPU v7x, 512 devices: a whole 4x8x8 slice. The times are simulated.
512 devices in a mesh: head: 8 (over z), seq: 64 (over y, x, core).
Axes of the slice: x: 4, y: 8, z: 8, core: 2. Of those that a mesh axis runs over, the one named last changes fastest.
Arguments:
- inputs: bfloat16 [8192, 2048], P('seq', 'head'), may hold values from -6 to 6
- w_query: bfloat16 [2048, 1024], P('seq', 'head'), may hold values from -0.125 to 0.125
- w_key: bfloat16 [2048, 1024], P('seq', 'head'), may hold values from -0.125 to 0.125
- w_value: bfloat16 [2048, 1024], P('seq', 'head'), may hold values from -0.125 to 0.125
- w_beta: bfloat16 [2048, 8], P('seq', 'head'), may hold values from -0.125 to 0.125
- beta_bias: float32 [8], P('head'), may hold values from -1.5 to 1.5
- cotangent: float32 [8192, 1024], P('seq', 'head'), may hold values from -6 to 6
Outputs:
- readout: float32 [8192, 1024], P('seq', 'head')
- grad_query: float32 [2048, 1024], P('seq', 'head')
- grad_key: float32 [2048, 1024], P('seq', 'head')
- grad_value: float32 [2048, 1024], P('seq', 'head')
- grad_beta: float32 [2048, 8], P('seq', 'head')
All inputs are finite; a program needn't handle non-finite values.
Results may differ from a plain program's by a relative error of at most 0.00305.
Values may be sent and summed in bfloat16 or wider, within the bound.
A program may use at most 64 MiB of HBM per device.

v0:
```python
import math

import jax
import jax.numpy as jnp
from jax import lax
from jax.sharding import PartitionSpec as P

BLOCK = 64


HIGHEST = lax.Precision.HIGHEST


def entering(part, axis, combine, identity, reverse):
    count = lax.axis_size(axis)
    place = lax.axis_index(axis)
    ahead = count - 1 - place if reverse else place
    gathered = jax.tree.map(lambda a: lax.all_gather(a, axis), part)
    state = jax.tree.map(lambda a, e: jnp.zeros_like(a) + jnp.asarray(e, a.dtype), part, identity)

    def one(turn, state):
        source = count - 1 - turn if reverse else turn
        return combine(
            state, jax.tree.map(lambda a: lax.dynamic_index_in_dim(a, source, 0, False), gathered)
        )

    return lax.fori_loop(0, ahead, one, state)


def unit_rows(raw, head_count):
    rows = raw.reshape(raw.shape[0], head_count, -1)
    scale_sq = jnp.mean(rows * rows, axis=-1, keepdims=True) + 1e-06
    return rows * lax.rsqrt(scale_sq) / math.sqrt(rows.shape[-1])


def blocked(rows):
    return rows.reshape(rows.shape[0] // BLOCK, BLOCK, rows.shape[1], rows.shape[2]).transpose(
        0, 2, 1, 3
    )


def wy_factors(key_blk, value_blk, beta_blk):
    key_beta = key_blk * beta_blk[..., None]
    value_beta = value_blk * beta_blk[..., None]
    gram_mat = jnp.einsum("...cd,...ed->...ce", key_beta, key_blk, precision=HIGHEST)
    lower_tri = jnp.tril(gram_mat, -1) + jnp.eye(key_blk.shape[-2], dtype=jnp.float32)
    solved = jax.scipy.linalg.solve_triangular(
        lower_tri, jnp.concatenate([key_beta, value_beta], axis=-1), lower=True, unit_diagonal=True
    )
    width = key_blk.shape[-1]
    return (solved[..., :width], solved[..., width:])


def block_step(carry_state, inputs_blk):
    query_blk, key_blk, value_blk, beta_blk = inputs_blk
    w_mat, u_mat = wy_factors(key_blk, value_blk, beta_blk)
    fresh_vals = u_mat - jnp.einsum("hcd,hvd->hcv", w_mat, carry_state, precision=HIGHEST)
    scores = jnp.tril(jnp.einsum("hcd,hed->hce", query_blk, key_blk, precision=HIGHEST))
    readout = jnp.einsum("hcd,hvd->hcv", query_blk, carry_state, precision=HIGHEST) + jnp.einsum(
        "hce,hev->hcv", scores, fresh_vals, precision=HIGHEST
    )
    new_state = carry_state + jnp.einsum("hcv,hcd->hvd", fresh_vals, key_blk, precision=HIGHEST)
    return (new_state, readout)


def beta_blocks(gate_logit, beta_bias):
    beta_rows = 2.0 * jax.nn.sigmoid(gate_logit + beta_bias[None, :])
    return blocked(beta_rows[..., None])[..., 0]


def sweep(query_raw, key_raw, value_raw, gate_logit, beta_bias, start_state):
    head_count = beta_bias.shape[0]
    query_all = blocked(unit_rows(query_raw, head_count))
    key_all = blocked(unit_rows(key_raw, head_count))
    value_all = blocked(value_raw.reshape(value_raw.shape[0], head_count, -1))
    beta_all = beta_blocks(gate_logit, beta_bias)
    end_state, outputs = lax.scan(
        block_step, start_state, (query_all, key_all, value_all, beta_all)
    )
    readout = outputs.transpose(0, 2, 1, 3).reshape(query_raw.shape[0], -1)
    return (readout, end_state)


def compose(earlier, later):
    decay = jnp.einsum("hij,hjk->hik", earlier[0], later[0], precision=HIGHEST)
    inflow = jnp.einsum("hij,hjk->hik", earlier[1], later[0], precision=HIGHEST) + later[1]
    return (decay, inflow)


def device_pair(key_raw, value_raw, gate_logit, beta_bias, eye_mat):
    head_count = beta_bias.shape[0]
    key_all = blocked(unit_rows(key_raw, head_count))
    value_all = blocked(value_raw.reshape(value_raw.shape[0], head_count, -1))
    beta_all = beta_blocks(gate_logit, beta_bias)
    w_mat, u_mat = wy_factors(key_all, value_all, beta_all)
    decays = eye_mat[None] - jnp.einsum("bhcd,bhce->bhde", w_mat, key_all, precision=HIGHEST)
    inflows = jnp.einsum("bhcv,bhcd->bhvd", u_mat, key_all, precision=HIGHEST)

    def absorb(pair_now, step_pair):
        return (compose(pair_now, step_pair), None)

    pair_end, unused = lax.scan(absorb, (eye_mat, jnp.zeros_like(eye_mat)), (decays, inflows))
    return pair_end


def per_device(inputs, w_query, w_key, w_value, w_beta, beta_bias, cotangent):
    x_full = lax.all_gather(inputs, "head", axis=1, tiled=True)
    head_count = beta_bias.shape[0]
    col_count = w_query.shape[1]
    width = col_count // head_count
    pieces = (
        lax.all_gather(w_query, "seq", axis=0, tiled=True),
        lax.all_gather(w_key, "seq", axis=0, tiled=True),
        lax.all_gather(w_value, "seq", axis=0, tiled=True),
        lax.all_gather(w_beta, "seq", axis=0, tiled=True),
    )
    x_block = x_full
    query_raw, key_raw, value_raw, gate_logit = tuple(
        (jnp.dot(x_block, piece, preferred_element_type=jnp.float32) for piece in pieces)
    )
    eye_mat = jnp.broadcast_to(jnp.eye(width, dtype=jnp.float32), (head_count, width, width))
    zero_state = jnp.zeros((head_count, width, width), jnp.float32)
    pair_dev = device_pair(key_raw, value_raw, gate_logit, beta_bias, eye_mat)
    prefix_pair = entering(pair_dev, "seq", compose, (eye_mat, zero_state), False)
    state_in = prefix_pair[1]

    def local_sweep(query_in, key_in, value_in, logit_in, state_start):
        return sweep(query_in, key_in, value_in, logit_in, beta_bias, state_start)

    primal_out, pullback = jax.vjp(local_sweep, query_raw, key_raw, value_raw, gate_logit, state_in)
    readout = primal_out[0]
    first_parts = pullback((cotangent, jnp.zeros_like(primal_out[1])))
    carried = first_parts[4]
    adjoint_pair = entering(
        (jnp.swapaxes(pair_dev[0], 1, 2), carried), "seq", compose, (eye_mat, zero_state), True
    )
    state_grad = adjoint_pair[1]
    second_parts = pullback((jnp.zeros_like(readout), state_grad))
    grad_parts = tuple((first_parts[index] + second_parts[index] for index in range(4)))
    grad_rounded = tuple((grad_term.astype(jnp.bfloat16) for grad_term in grad_parts))
    x_cols = lax.all_to_all(x_full, "seq", split_axis=1, concat_axis=0, tiled=True)
    pieces = (
        lax.all_gather(grad_rounded[0], "seq", axis=0, tiled=True),
        lax.all_gather(grad_rounded[1], "seq", axis=0, tiled=True),
        lax.all_gather(grad_rounded[2], "seq", axis=0, tiled=True),
        lax.all_gather(grad_rounded[3], "seq", axis=0, tiled=True),
    )
    x_block = x_cols
    results = tuple(
        (
            jnp.einsum("td,tc->dc", x_block, piece, preferred_element_type=jnp.float32)
            for piece in pieces
        )
    )
    return (readout, results[0], results[1], results[2], results[3])


def solution(mesh):
    return jax.shard_map(
        per_device,
        mesh=mesh,
        in_specs=(
            P("seq", "head"),
            P("seq", "head"),
            P("seq", "head"),
            P("seq", "head"),
            P("seq", "head"),
            P("head"),
            P("seq", "head"),
        ),
        out_specs=(
            P("seq", "head"),
            P("seq", "head"),
            P("seq", "head"),
            P("seq", "head"),
            P("seq", "head"),
        ),
        check_vma=False,
    )
```

profile of v0, /device:TPU:1, one launch (start us, length us, event | category | flops | bytes accessed | tf_op | source)
XLA Modules:
  0.0 1106.9 jit_solution(4734290244855063951)
XLA Ops:
  8.3 28.5 %all_gather.51 = bf16[128,2048]{0,1:T(8,128)(2,1)} all-gather(bf16[128,256]{0,1:T(8,128)(2,1)S(1)} %copy.48), channel_id=1, replica_groups=mesh['head'=8,'seq'=64] {'head'}, dimensions={1}, use_global_device_ids=true | all-gather | bytes 589824 | tf_op jit(solution)/shard_map/all_gather | solution.py:107
  36.7 58.1 %all_gather.52 = bf16[2048,128]{1,0:T(8,128)(2,1)S(1)} all-gather(bf16[32,128]{1,0:T(8,128)(2,1)} %param.25), channel_id=1, replica_groups=mesh['head'=8,'seq'=64] {'seq'}, dimensions={0}, use_global_device_ids=true | all-gather | bytes 532480 | tf_op jit(solution)/shard_map/all_gather | solution.py:113
  99.1 123.7 %all-reduce.4 = bf16[2048]{0:T(1024)(128)(2,1)S(1)} all-reduce(bf16[2048]{0:T(1024)(128)(2,1)S(1)} %dynamic-update-slice), channel_id=1, replica_groups=mesh['head'=8,'seq'=64] {'seq'}, use_global_device_ids=true, to_apply=%add.4 | all-reduce | flops 2048 | bytes 8192 | tf_op jit(solution)/shard_map/reshape.130
  224.1 50.2 %all_gather.54 = bf16[2048,128]{1,0:T(8,128)(2,1)S(1)} all-gather(bf16[32,128]{1,0:T(8,128)(2,1)S(1)} %copy-done.4), channel_id=1, replica_groups=mesh['head'=8,'seq'=64] {'seq'}, dimensions={0}, use_global_device_ids=true | all-gather | bytes 532480 | tf_op jit(solution)/shard_map/all_gather | solution.py:114
  276.1 9.8 custom-call.17
  291.2 50.1 %all_gather.59 = bf16[2048,128]{1,0:T(8,128)(2,1)S(1)} all-gather(bf16[32,128]{1,0:T(8,128)(2,1)S(1)} %copy-done.5), channel_id=1, replica_groups=mesh['head'=8,'seq'=64] {'seq'}, dimensions={0}, use_global_device_ids=true | all-gather | bytes 532480 | tf_op jit(solution)/shard_map/all_gather | solution.py:112
  342.8 27.6 %all-gather.20.cloned.1.call-done = f32[64,128,128]{2,1,0:T(8,128)} async-done(((f32[1,128,128]{2,1,0:T(8,128)}), f32[64,128,128]{2,1,0:T(8,128)}) %all-gather.20.cloned.1.call-update) | async-done | bytes 4194320 | tf_op jit(solution)/shard_map/all_gather | solution.py:18
  370.5 85.3 %all-gather.22.cloned.1.call-done = f32[64,128,128]{2,1,0:T(8,128)} async-done(((f32[1,128,128]{2,1,0:T(8,128)}), f32[64,128,128]{2,1,0:T(8,128)}) %all-gather.22.cloned.1.call-update) | async-done | bytes 4194320 | tf_op jit(solution)/shard_map/all_gather | solution.py:18
  458.0 13.8 %while.125 = (s32[]{:T(128)}, f32[1,128,128]{2,1,0:T(8,128)S(1)}, f32[2,1,64,128]{3,2,1,0:T(8,128)S(1)}, f32[2,1,64,1]{2,3,1,0:T(1,128)S(1)}, f32[2,1,64,128]{3,...) while((s32[]{:T(128)}, f32[1,128,128]{2,1,0:T(8,128)S(1)}, ...), condition=%wide.region_7.8_spmd.clone, body=%wide.region_6.7_spmd.clone.sunk | while | flops 69337152 | bytes 1579981 | solution.py:77
  458.7 4.9 custom-call.30
  465.6 4.9 custom-call.30
  472.4 17.3 %while.127 = (s32[]{:T(128)}, f32[1,128,128]{2,1,0:T(8,128)S(1)}, f32[2,1,64,128]{3,2,1,0:T(8,128)S(1)}, f32[2,1,64,128]{3,2,1,0:T(8,128)S(1)}, f32[2,1,64,128]{...) while((s32[]{:T(128)}, f32[1,128,128]{2,1,0:T(8,128)S(1)}, ...), condition=%wide.region_11.13_spmd.clone.clone.clone, body=%wide.region_8.12_spmd.clone.clone.clone.sunk | while | flops 141836288 | bytes 2224647 | solution.py:77
  473.5 4.9 custom-call.32
  482.1 4.9 custom-call.32
  490.5 50.8 %all-gather.24.cloned.1.call-done = f32[64,128,128]{2,1,0:T(8,128)} async-done(((f32[1,128,128]{2,1,0:T(8,128)}), f32[64,128,128]{2,1,0:T(8,128)}) %all-gather.24.cloned.1.call-update) | async-done | bytes 4194320 | tf_op jit(solution)/shard_map/all_gather | solution.py:18
  541.2 160.5 %all-gather.26.cloned.1.call-done = f32[64,128,128]{2,1,0:T(8,128)} async-done(((f32[1,128,128]{2,1,0:T(8,128)}), f32[64,128,128]{2,1,0:T(8,128)}) %all-gather.26.cloned.1.call-update) | async-done | bytes 4194320 | tf_op jit(solution)/shard_map/all_gather | solution.py:18
  701.8 131.2 %while.124 = (s32[]{:T(128)}, f32[1,128,128]{1,2,0:T(8,128)S(1)}, s32[]{:T(128)}, f32[64,1,128,128]{3,2,1,0:T(8,128)}, f32[64,1,128,128]{3,2,0,1:T(8,128)}, /*index=5*/s32[]{:T(128)}, s32[]{:T(128)}, s32[]{:T(128)}, s32[]{:T(128)}) while((s32[]{:T(128)}, f32[1,128,128]{1,2,0:T(8,128)S(1)}, s32[]{:T(128)}, f32[64,1,128,128]{3,2,1,0:T(8,128)}, ...), condition=%wide.region_14.16_spmd, body=%wide.region_13.15_spmd.sunk | while | flops 25182212 | bytes 655515 | solution.py:27
  833.2 16.4 %while.126 = (s32[]{:T(128)}, f32[1,128,128]{2,1,0:T(8,128)S(1)}, f32[2,1,64,128]{3,2,1,0:T(8,128)S(1)}, f32[2,1,64,128]{3,2,1,0:T(8,128)S(1)}, f32[2,1,64,128]{...) while((s32[]{:T(128)}, f32[1,128,128]{2,1,0:T(8,128)S(1)}, ...), condition=%wide.region_20.22_spmd.clone.clone, body=%wide.region_15.21_spmd.clone.clone.sunk | while | flops 122937152 | bytes 1877245 | solution.py:77
  834.0 4.9 custom-call.31
  852.1 6.4 all-to-all-start
  858.7 44.7 %all-gather.5 = bf16[64,1,128]{2,1,0:T(2,128)(2,1)S(1)} all-gather(bf16[1,1,128]{2,1,0:T(2,128)(2,1)S(1)} %convert_bitcast_fusion), channel_id=6, replica_groups=mesh['head'=8,'seq'=64] {'seq'}, dimensions={0}, use_global_device_ids=true | all-gather | bytes 16640 | tf_op jit(solution)/shard_map/all_gather | solution.py:146
  904.2 25.4 %all-gather.14.cloned.1.call-done = bf16[8192,128]{1,0:T(8,128)(2,1)} async-done(((bf16[128,128]{1,0:T(8,128)(2,1)}), bf16[8192,128]{1,0:T(8,128)(2,1)}) %all-gather.14.cloned.1.call-update) | async-done | bytes 2097168 | tf_op jit(solution)/shard_map/all_gather | solution.py:143
  932.3 81.2 %all-gather.16.cloned.1.call-done = bf16[8192,128]{1,0:T(8,128)(2,1)} async-done(((bf16[128,128]{1,0:T(8,128)(2,1)}), bf16[8192,128]{1,0:T(8,128)(2,1)}) %all-gather.16.cloned.1.call-update) | async-done | bytes 2097168 | tf_op jit(solution)/shard_map/all_gather | solution.py:144
  1016.1 81.3 %all-gather.18.cloned.1.call-done = bf16[8192,128]{1,0:T(8,128)(2,1)} async-done(((bf16[128,128]{1,0:T(8,128)(2,1)}), bf16[8192,128]{1,0:T(8,128)(2,1)}) %all-gather.18.cloned.1.call-update) | async-done | bytes 2097168 | tf_op jit(solution)/shard_map/all_gather | solution.py:145
  (474 shorter events, 183.0 us)
Async XLA Ops:
  7.2 91.7 %copy-start.6 = (bf16[32,1]{0,1:T(2,128)(2,1)S(1)}, bf16[32,1]{0,1:T(2,128)(2,1)}, u32[]{:S(2)}) copy-start(bf16[32,1]{0,1:T(2,128)(2,1)} %param.27) | copy-start | bytes 196
  7.2 216.9 %copy-start.4 = (bf16[32,128]{1,0:T(8,128)(2,1)S(1)}, bf16[32,128]{1,0:T(8,128)(2,1)}, u32[]{:S(2)}) copy-start(bf16[32,128]{1,0:T(8,128)(2,1)} %param.26) | copy-start | bytes 24580
  7.2 363.3 %all-gather.20.cloned.1.call-start = ((), (), s32[]{:S(2)}) async-start(), calls=%async_computation.4 | async-start | bytes 4259840 | tf_op jit(solution)/shard_map/all_gather | solution.py:18
  287.2 4.0 copy-start.5
  288.7 1.6 copy-start.2
  289.5 166.2 %all-gather.22.cloned.1.call-start = ((), (), s32[]{:S(2)}) async-start(), calls=%async_computation.5 | async-start | bytes 4259840 | tf_op jit(solution)/shard_map/all_gather | solution.py:18
  290.3 250.9 %all-gather.24.cloned.1.call-start = ((), (), s32[]{:S(2)}) async-start(), calls=%async_computation.6 | async-start | bytes 4259840 | tf_op jit(solution)/shard_map/all_gather | solution.py:18
  291.0 410.7 %all-gather.26.cloned.1.call-start = ((), (), s32[]{:S(2)}) async-start(), calls=%async_computation.7 | async-start | bytes 4259840 | tf_op jit(solution)/shard_map/all_gather | solution.py:18
  458.0 13.9 %copy-start.1 = (f32[128,128]{1,0:T(8,128)S(1)}, f32[128,128]{1,0:T(8,128)}, u32[]{:S(2)}) copy-start(f32[128,128]{1,0:T(8,128)} %param.29) | copy-start | bytes 196612
  471.8 0.6 copy-start.3
  489.8 0.6 copy-start
  490.4 439.2 %all-gather.14.cloned.1.call-start = ((), (), s32[]{:S(2)}) async-start(), calls=%async_computation.1 | async-start | bytes 2129920 | tf_op jit(solution)/shard_map/all_gather | solution.py:143
  850.4 163.0 %all-gather.16.cloned.1.call-start = ((), (), s32[]{:S(2)}) async-start(), calls=%async_computation.2 | async-start | bytes 2129920 | tf_op jit(solution)/shard_map/all_gather | solution.py:144
  851.4 246.0 %all-gather.18.cloned.1.call-start = ((), (), s32[]{:S(2)}) async-start(), calls=%async_computation.3 | async-start | bytes 2129920 | tf_op jit(solution)/shard_map/all_gather | solution.py:145
  852.1 51.3 %all-to-all-start = ((bf16[128,64,32]{0,2,1:T(8,128)(2,1)}), bf16[128,64,32]{0,2,1:T(8,128)(2,1)S(1)}, u32[]{:S(2)}, u32[]{:S(2)}) async-start(bf16[128,64,32]{0,2,1:T(8,128)(2,1)} %bitcast.56), calls=%async_computation | async-start | bytes 1048576 | tf_op jit(solution)/shard_map/all_to_all | solution.py:141
Sparse Core Ops, SparseCore 0:
  289.6 80.8 all-gather.19
  373.8 81.8 all-gather.21
  459.1 82.0 all-gather.23
  544.4 157.2 all-gather.25
  850.6 79.0 all-gather.13
  932.8 80.5 all-gather.15
  1016.8 80.5 all-gather.17
where the time goes:
time: 1110 us
  waiting for transfers between devices  513 us (46%)
  blocking collectives  355 us (32%)
  matrix products  103 us (9%)
  local copies, waits for them, and re-layouts  65.4 us (6%)
  other arithmetic  43.8 us (4%)
  between operations  15.9 us (1%)
    all_gather x4, waiting for transfers between devices, entering(): gathered = jax.tree.map(lambda a: lax.all_gather(a, axis), part)  324 us
    another operation x1, blocking collectives  124 us
    all_gather x1, waiting for transfers between devices, per_device(): lax.all_gather(grad_rounded[2], 'seq', axis=0, tiled=True)  81.3 us
    all_gather x1, waiting for transfers between devices, per_device(): lax.all_gather(grad_rounded[1], 'seq', axis=0, tiled=True)  81.2 us
    dot_general x65, matrix products, compose(): jnp.einsum('hij,hjk->hik', earlier[1], later[0], precision=HIGHEST)  71.8 us
    dynamic_slice x126, local copies, waits for them, and re-layouts, one(): lax.dynamic_index_in_dim(a, source, 0, False)  59 us
    all_gather x1, blocking collectives, per_device(): lax.all_gather(w_key, 'seq', axis=0, tiled=True)  58.1 us
    all_gather x1, blocking collectives, per_device(): lax.all_gather(w_value, 'seq', axis=0, tiled=True)  50.2 us
  transfers between devices with their start and end apart: 8, of which 7 were waited for; matrix products, arithmetic and copies ran while one was open for 4% of the time, Pallas kernels for 0%

commit v1 on v0

v1 whole, which is shorter than its diff:
```python
import functools
import math

import jax
import jax.numpy as jnp
from jax import lax
from jax.experimental import pallas as pl
from jax.experimental.pallas import tpu as pltpu
from jax.sharding import PartitionSpec as P

MESH = pl.DeviceIdType.MESH
F32 = jnp.float32
BF16 = jnp.bfloat16
NN = (((1,), (0,)), ((), ()))
NT = (((1,), (1,)), ((), ()))


def split(a):
    high = a.astype(BF16)
    return high, (a - high.astype(F32)).astype(BF16)


def mm(a, b, form=NN):
    a_high, a_low = split(a)
    b_high, b_low = split(b)
    return mm1(a_high, b_high, form) + (mm1(a_high, b_low, form) + mm1(a_low, b_high, form))


def mm1(a, b, form=NN):
    return lax.dot_general(a, b, form, preferred_element_type=F32)


def kernel(
    nz, ny, nj,
    x_ref, wq_ref, wk_ref, wv_ref, wb_ref, bias_ref, cot_ref,
    o_ref, gq_ref, gk_ref, gv_ref, gb_ref,
    wg, xg, xt, xr, ag, bcs, bcr, gbc, ya, ybc, sgs, sgr, ggs, gg, gbs, gbr, ps, pr, pbs, pbr,
    zs, zr, w1s, w1r, w2s, w2r, w3s, w3r, as_, ar, ass, asr, bs, br, y1s, y1r, y2s, y2r, y3s, y3r,
    xs, xrs, ss, sr, gs, grs, ps_, prs, pbs_, pbrs,
):
    h = lax.axis_index("head")
    s = lax.axis_index("seq")
    y = s // nj
    j = lax.rem(s, nj)
    core = lax.rem(j, 2)
    tok, fb = x_ref.shape
    rw, width = wq_ref.shape
    vp = width // nj

    def zdev(d):
        return (lax.rem(h + d + nz, nz), s)

    def yat(d):
        return lax.rem(y + d + ny, ny)

    def ydev(d):
        return (h, yat(d) * nj + j)

    def jat(d):
        return lax.rem(j + d + nj, nj)

    def jdev(d):
        return (h, y * nj + jat(d))

    sib = j + 1 - 2 * core
    sibdev = (h, y * nj + sib)
    sent = []

    def push(src, dst, ssem, rsem, dev):
        copy = pltpu.make_async_remote_copy(
            src_ref=src, dst_ref=dst, send_sem=ssem, recv_sem=rsem, device_id=dev, device_id_type=MESH
        )
        copy.start()
        sent.append(copy)

    def arrived(dst, ssem, rsem):
        pltpu.make_async_remote_copy(
            src_ref=dst, dst_ref=dst, send_sem=ssem, recv_sem=rsem, device_id=sibdev, device_id_type=MESH
        ).wait_recv()

    barrier = pltpu.get_barrier_semaphore()
    for d in range(1, nz):
        pl.semaphore_signal(barrier, inc=1, device_id=zdev(d), device_id_type=MESH)
    for d in range(1, ny):
        pl.semaphore_signal(barrier, inc=1, device_id=ydev(d), device_id_type=MESH)
    for d in range(1, nj):
        pl.semaphore_signal(barrier, inc=1, device_id=jdev(d), device_id_type=MESH)

    wg[j, y, 0:rw, :] = wq_ref[...]
    wg[j, y, rw:2 * rw, :] = wk_ref[...]
    wg[j, y, 2 * rw:3 * rw, :] = wv_ref[...]
    lane = lax.broadcasted_iota(jnp.int32, (rw, 128), 1)
    row = lax.broadcasted_iota(jnp.int32, (rw, 128), 0)
    put = lane == lax.rem(j * rw, 128) + row
    wb_row = jnp.sum(jnp.where(put, wb_ref[...].astype(F32), 0.0), axis=0, keepdims=True)
    wg[j, y, 3 * rw:3 * rw + 16, :] = jnp.broadcast_to(wb_row, (16, 128)).astype(BF16)
    xg[h] = x_ref[...]

    pl.semaphore_wait(barrier, nz + ny + nj - 3)

    order_z = sorted(range(1, nz), key=lambda d: min(d, nz - d))
    order_y = sorted(range(1, ny), key=lambda d: min(d, ny - d))
    order_j = sorted(range(1, nj), key=lambda d: min(d, nj - d))
    evens = [e for e in order_j if e % 2 == 0]

    for d in order_y:
        push(wg.at[j, y], wg.at[j, y], w1s.at[d], w1r.at[d], ydev(d))
    for n, e in enumerate(evens):
        push(wg.at[j, y], wg.at[j, y], w2s.at[n, 0], w2r.at[n, 0], jdev(e))
    for d in order_z:
        push(xg.at[h], xg.at[h], zs.at[d], zr.at[d], zdev(d))
    for d in order_y:
        part = wg.at[j, yat(-d)]
        arrived(part, w1s.at[d], w1r.at[d])
        for n, e in enumerate(evens):
            push(part, part, w2s.at[n, d], w2r.at[n, d], jdev(e))
    push(wg.at[j], wg.at[j], w3s.at[0], w3r.at[0], sibdev)

    cot = cot_ref[...]
    cot_t = cot.T

    for d in order_z:
        arrived(xg.at[lax.rem(h - d + nz, nz)], zs.at[d], zr.at[d])
    for n, e in enumerate(evens):
        col = wg.at[jat(-e)]
        for d in [0] + order_y:
            arrived(wg.at[jat(-e), yat(-d)], w2s.at[n, d], w2r.at[n, d])
        push(col, col, w3s.at[n + 1], w3r.at[n + 1], sibdev)
    arrived(wg.at[sib], w3s.at[0], w3r.at[0])
    for n, e in enumerate(evens):
        arrived(wg.at[lax.rem(sib - e + nj, nj)], w3s.at[n + 1], w3r.at[n + 1])

    raw = jnp.zeros((tok, 3 * width), F32)
    lacc = jnp.zeros((tok, 128), F32)
    per = 128 // rw
    for b in range(nz):
        xb = xg[b]
        w_b = jnp.concatenate(
            [wg[:, b, m * rw:(m + 1) * rw, :].reshape(fb, width) for m in range(3)], axis=1
        )
        raw = raw + mm1(xb, w_b)
        for g in range(fb // 128):
            w_row = jnp.sum(wg[g * per:(g + 1) * per, b, 3 * rw:3 * rw + 16, :].astype(F32), axis=0)[:1]
            lacc = lacc + xb[:, g * 128:(g + 1) * 128].astype(F32) * w_row
    logit = jnp.sum(lacc, axis=1, keepdims=True) + bias_ref[0]
    beta = 2.0 * jax.nn.sigmoid(logit)

    def unit(r):
        scale = lax.rsqrt(jnp.mean(r * r, axis=1, keepdims=True) + 1e-06) * (1.0 / math.sqrt(width))
        return r * scale, scale

    q, q_scale = unit(raw[:, :width])
    k, k_scale = unit(raw[:, width:2 * width])
    v = raw[:, 2 * width:]

    ri = lax.broadcasted_iota(jnp.int32, (tok, tok), 0)
    ci = lax.broadcasted_iota(jnp.int32, (tok, tok), 1)
    lower = ri > ci
    upper = ri < ci
    lower_d = ri >= ci
    upper_d = ri <= ci
    eye = jnp.where(ri == ci, 1.0, 0.0).astype(F32)

    gram = mm(k, k, NT)
    low = jnp.where(lower, beta * gram, 0.0)
    t_mat = eye - jnp.where((ri // 2) == (ci // 2), low, 0.0)
    size = 2
    while size < tok:
        level = ((ri // (2 * size)) == (ci // (2 * size))) & ((ri // size) != (ci // size))
        t_mat = t_mat - mm(t_mat, mm(jnp.where(level, low, 0.0), t_mat))
        size *= 2
    wu = mm(t_mat, jnp.concatenate([beta * k, beta * v], axis=1))
    w_mat, u_mat = wu[:, :width], wu[:, width:]
    m_mat = jnp.where(lower_d, mm(q, k, NT), 0.0)
    mwu = mm(m_mat, wu)
    q_eff = q - mwu[:, :width]
    m_u = mwu[:, width:]
    kwu = mm(k.T, wu)
    ag[j] = eye - kwu[:, :width]
    bcs[:, 0] = kwu[:, width:].T.reshape(nj, vp, width)
    bcs[:, 1] = mm(cot_t, q_eff).reshape(nj, vp, width)
    bcr[j] = bcs[j]

    push(ag.at[j], ag.at[j], ass.at[0], asr.at[0], sibdev)
    for n, e in enumerate(evens):
        push(ag.at[j], ag.at[j], as_.at[n], ar.at[n], jdev(e))
    for d in order_j:
        push(bcs.at[jat(d)], bcr.at[j], bs.at[d], br.at[d], jdev(d))

    m_t = jnp.where(upper_d, mm(k, q, NT), 0.0)
    ty = mm(t_mat.T, jnp.concatenate([k, mm(m_t, cot)], axis=1))
    t_k, y_0 = ty[:, :width], ty[:, width:]
    for b in range(nz):
        xt[:, b * rw:(b + 1) * rw, :] = xg[b].astype(F32).T.astype(BF16).reshape(nj, rw, tok)

    for n, e in enumerate(evens):
        part = ag.at[jat(-e)]
        arrived(part, as_.at[n], ar.at[n])
        push(part, part, ass.at[n + 1], asr.at[n + 1], sibdev)
    arrived(ag.at[sib], ass.at[0], asr.at[0])
    for n, e in enumerate(evens):
        arrived(ag.at[lax.rem(sib - e + nj, nj)], ass.at[n + 1], asr.at[n + 1])
    for d in order_j:
        arrived(bcr.at[jat(-d)], bs.at[d], br.at[d])

    p_mat = ag[0]
    b_row = bcr[0, 0]
    c_row = bcr[nj - 1, 1]
    befores = [None, p_mat]
    b_before = [None, b_row]
    c_after = {nj - 2: c_row}
    for i in range(1, nj):
        p_mat = mm(ag[i], p_mat)
        b_row = mm(b_row, ag[i], NT) + bcr[i, 0]
        c_row = mm(c_row, ag[nj - 1 - i]) + bcr[nj - 1 - i, 1]
        befores.append(p_mat)
        b_before.append(b_row)
        c_after[nj - 2 - i] = c_row
    ybc[y] = jnp.zeros((vp, width), F32)
    gbc[0] = b_row
    gbc[1] = c_row
    half = tok // 2
    top, bottom = p_mat[:half].astype(BF16), p_mat[half:].astype(BF16)
    ya[core, y] = jnp.where(core == 0, top, bottom)
    for d in order_y:
        push(ya.at[core, y], ya.at[core, y], y1s.at[d], y1r.at[d], ydev(d))
        side = (y + d) // ny
        push(gbc.at[side], ybc.at[y], y2s.at[d], y2r.at[d], ydev(d))
    for d in order_j:
        xr_dst = xr.at[j]
        push(xt.at[jat(d)], xr_dst, xs.at[d], xrs.at[d], jdev(d))
    xr[j] = xt[j]

    afters = {nj - 2: ag[nj - 1]}
    for i in range(nj - 3, -1, -1):
        afters[i] = mm(afters[i + 1], ag[i + 1])

    for d in order_y:
        arrived(ya.at[core, yat(-d)], y1s.at[d], y1r.at[d])
    push(ya.at[core], ya.at[core], y3s, y3r, sibdev)
    for d in order_y:
        arrived(ybc.at[yat(-d)], y2s.at[d], y2r.at[d])
    arrived(ya.at[1 - core], y3s, y3r)

    def full(t):
        return jnp.concatenate([ya[0, t], ya[1, t]], axis=0).astype(F32)

    s_g = jnp.zeros((vp, width), F32)
    g_g = jnp.zeros((vp, width), F32)
    for t in range(ny - 1):
        s_g = jnp.where(t < y, mm(s_g, full(t), NT) + ybc[t], s_g)
        u = ny - 1 - t
        g_g = jnp.where(u > y, mm(g_g, full(u)) + ybc[u], g_g)

    sgs[0, 0] = s_g
    sgs[nj - 1, 1] = g_g
    for i in range(1, nj):
        sgs[i, 0] = mm(s_g, befores[i], NT) + b_before[i]
    for i in range(nj - 1):
        sgs[i, 1] = mm(g_g, afters[i]) + c_after[i]
    for d in order_j:
        push(sgs.at[jat(d)], sgr.at[j], ss.at[d], sr.at[d], jdev(d))
    sgr[j] = sgs[j]
    for d in order_j:
        arrived(sgr.at[jat(-d)], ss.at[d], sr.at[d])

    state = sgr[:, 0].reshape(width, width)
    grad = sgr[:, 1].reshape(width, width)
    y_mat = y_0 + mm(t_k, grad, NT)
    b_y = beta * y_mat
    ggs[2] = b_y.astype(BF16)

    def share(m):
        for d in order_j:
            push(ggs.at[m], gg.at[j, m], gs.at[m, d], grs.at[m, d], jdev(d))
        gg[j, m] = ggs[m]

    share(2)
    fresh = u_mat - mm(w_mat, state, NT)
    o_ref[...] = mm(q_eff, state, NT) + m_u
    d_m = jnp.where(lower_d, mm(cot, fresh, NT), 0.0)
    d_q = mm(cot, state) + mm(d_m, k)
    ggs[0] = (q_scale * (d_q - q * jnp.sum(d_q * q, axis=1, keepdims=True))).astype(BF16)
    share(0)
    rest = v - mm(k, state, NT)
    d_mt = jnp.where(upper_d, mm(fresh, cot, NT), 0.0)
    yd = jnp.where(lower, mm(y_mat, fresh, NT), 0.0)
    both = beta * yd + jnp.where(upper, mm(fresh, b_y, NT), 0.0)
    d_k = mm(fresh, grad) - mm(b_y, state) + mm(d_mt, q) - mm(both, k)
    ggs[1] = (k_scale * (d_k - k * jnp.sum(d_k * k, axis=1, keepdims=True))).astype(BF16)
    share(1)
    d_beta = jnp.sum(y_mat * rest - yd * gram, axis=1, keepdims=True)
    d_logit = d_beta * beta * (1.0 - 0.5 * beta)
    dl_row = jnp.sum(eye * d_logit, axis=0, keepdims=True)
    gbs[...] = jnp.broadcast_to(dl_row, (16, tok)).astype(BF16)
    for d in order_j:
        push(gbs, gbr.at[j], gs.at[3, d], grs.at[3, d], jdev(d))
    gbr[j] = gbs[...]

    for d in order_j:
        arrived(xr.at[jat(-d)], xs.at[d], xrs.at[d])
    x_t = jnp.concatenate([xr[i] for i in range(nj)], axis=1)

    outs = {0: gq_ref, 1: gk_ref, 2: gv_ref}
    for m in (2, 0, 1):
        for d in order_j:
            arrived(gg.at[jat(-d), m], gs.at[m, d], grs.at[m, d])
        part = mm1(x_t, gg[:, m].reshape(nj * tok, width)).reshape(ny, rw, width)
        pr[m, y] = jnp.zeros((rw, width), BF16)
        ps[m] = part.astype(BF16)
        for d in order_y:
            push(ps.at[m, yat(d)], pr.at[m, y], ps_.at[m, d], prs.at[m, d], ydev(d))
        for t in range(ny):
            @pl.when(t == y)
            def _():
                outs[m][...] = part[t]
    for d in order_j:
        arrived(gbr.at[jat(-d)], gs.at[3, d], grs.at[3, d])
    pb = mm1(jnp.concatenate([gbr[i] for i in range(nj)], axis=1), x_t, NT)
    for g in range(fb // 128):
        pbs[g] = pb[:8, g * 128:(g + 1) * 128]
    for d in order_y:
        push(pbs.at[yat(d) * rw // 128], pbr.at[y], pbs_.at[d], pbrs.at[d], ydev(d))
    pbr[y] = pbs[y * rw // 128]

    for m in (2, 0, 1):
        for d in order_y:
            arrived(pr.at[m, yat(-d)], ps_.at[m, d], prs.at[m, d])
        outs[m][...] += jnp.sum(pr[m].astype(F32), axis=0)
    for d in order_y:
        arrived(pbr.at[yat(-d)], pbs_.at[d], pbrs.at[d])
    pb_row = jnp.sum(pbr[...], axis=0)[:1]
    take = lane == lax.rem(y * rw, 128) + row
    gb_ref[...] = jnp.sum(jnp.where(take, pb_row, 0.0), axis=1, keepdims=True)

    for copy in sent:
        copy.wait_send()


def per_device(mesh, *args):
    inputs, w_query, w_key, w_value, w_beta, beta_bias, cotangent = args
    nz = mesh.shape["head"]
    ny = nz
    nj = mesh.shape["seq"] // ny
    tok, fb = inputs.shape
    rw, width = w_query.shape
    vp = width // nj
    ne = nj // 2
    vmem = pl.BlockSpec(memory_space=pltpu.VMEM)
    dma = pltpu.SemaphoreType.DMA
    scratch = [
        pltpu.VMEM((nj, ny, 3 * rw + 16, 128), BF16),
        pltpu.VMEM((nz, tok, fb), BF16),
        pltpu.VMEM((nj, nz * rw, tok), BF16),
        pltpu.VMEM((nj, nz * rw, tok), BF16),
        pltpu.VMEM((nj, width, width), F32),
        pltpu.VMEM((nj, 2, vp, width), F32),
        pltpu.VMEM((nj, 2, vp, width), F32),
        pltpu.VMEM((2, vp, width), F32),
        pltpu.VMEM((2, ny, width // 2, width), BF16),
        pltpu.VMEM((ny, vp, width), F32),
        pltpu.VMEM((nj, 2, vp, width), F32),
        pltpu.VMEM((nj, 2, vp, width), F32),
        pltpu.VMEM((3, tok, width), BF16),
        pltpu.VMEM((nj, 3, tok, width), BF16),
        pltpu.VMEM((16, tok), BF16),
        pltpu.VMEM((nj, 16, tok), BF16),
        pltpu.VMEM((3, ny, rw, width), BF16),
        pltpu.VMEM((3, ny, rw, width), BF16),
        pltpu.VMEM((fb // 128, 8, 128), F32),
        pltpu.VMEM((ny, 8, 128), F32),
        dma((nz,)), dma((nz,)),
        dma((ny,)), dma((ny,)),
        dma((ne, ny)), dma((ne, ny)),
        dma((ne,)), dma((ne,)),
        dma((ne,)), dma((ne,)),
        dma((ne,)), dma((ne,)),
        dma((nj,)), dma((nj,)),
        dma((ny,)), dma((ny,)),
        dma((ny,)), dma((ny,)),
        dma, dma,
        dma((nj,)), dma((nj,)),
        dma((nj,)), dma((nj,)),
        dma((4, nj)), dma((4, nj)),
        dma((3, ny)), dma((3, ny)),
        dma((ny,)), dma((ny,)),
    ]
    return pl.pallas_call(
        functools.partial(kernel, nz, ny, nj),
        out_shape=(
            jax.ShapeDtypeStruct((tok, width), F32),
            jax.ShapeDtypeStruct((rw, width), F32),
            jax.ShapeDtypeStruct((rw, width), F32),
            jax.ShapeDtypeStruct((rw, width), F32),
            jax.ShapeDtypeStruct((rw, 1), F32),
        ),
        in_specs=[vmem, vmem, vmem, vmem, vmem, pl.BlockSpec(memory_space=pltpu.SMEM), vmem],
        out_specs=(vmem,) * 5,
        scratch_shapes=scratch,
        compiler_params=pltpu.CompilerParams(
            collective_id=0, has_side_effects=True, vmem_limit_bytes=48 * 1024 * 1024
        ),
        name="delta_step",
    )(inputs, w_query, w_key, w_value, w_beta, beta_bias, cotangent)


def solution(mesh):
    return jax.shard_map(
        functools.partial(per_device, mesh),
        mesh=mesh,
        in_specs=(P("seq", "head"),) * 5 + (P("head"), P("seq", "head")),
        out_specs=(P("seq", "head"),) * 5,
        check_vma=False,
    )
```

time: 1110 us -> 84 us (0.08)
  waiting for transfers between devices: 513 us -> 0 us
  blocking collectives: 355 us -> 0 us
  matrix products: 103 us -> 0 us
  Pallas kernels: 0 us -> 76.1 us
  local copies, waits for them, and re-layouts: 65.4 us -> 6.21 us
  other arithmetic: 43.8 us -> 0 us
  between operations: 15.9 us -> 1.34 us
    all_gather x7 -> x0, waiting for transfers between devices: 512 us -> none  [the longest x4 324 us: entering(): gathered = jax.tree.map(lambda a: lax.all_gather(a, axis), part)]
    all_gather x5 -> x0, blocking collectives: 231 us -> none  [the longest x1 58.1 us: per_device(): lax.all_gather(w_key, 'seq', axis=0, tiled=True)]
    another operation x1 -> x0, blocking collectives: 124 us -> none
    dot_general x138 -> x0, matrix products: 101 us -> none  [the longest x65 71.8 us: compose(): jnp.einsum('hij,hjk->hik', earlier[1], later[0], precision=HIGHEST)]
    pallas_call x0 -> x1, Pallas kernels: none -> 76.1 us  [per_device(): pl.pallas_call(functools.partial(kernel, nz, ny, nj), out_shape=(jax.Shap...]
    dynamic_slice x130 -> x0, local copies, waits for them, and re-layouts: 59.2 us -> none  [the longest x126 59 us: one(): lax.dynamic_index_in_dim(a, source, 0, False)]
    another operation x28 -> x0, other arithmetic: 40 us -> none  [the longest x23 39.8 us: wy_factors(): jax.scipy.linalg.solve_triangular(lower_tri, jnp.concatenate([key_beta, v...]
  transfers between devices with their start and end apart: 8 -> 0, of which waited for: 7 -> 0; matrix products, arithmetic and copies ran while one was open for 4% -> 0% of each run, Pallas kernels for 0% -> 0%
where the time goes in v1:
time: 84 us; the launch traced here: 83.6 us
  Pallas kernels  76.1 us (91%)
  local copies, waits for them, and re-layouts  6.21 us (7%)
  between operations  1.34 us (2%)
    pallas_call x1, Pallas kernels, per_device(): pl.pallas_call(functools.partial(kernel, nz, ny, nj), out_shape=(jax.Shap...  76.1 us
    unnamed x17, local copies, waits for them, and re-layouts  5.63 us

profile of v1, /device:TPU:1, one launch (start us, length us, event | category | flops | bytes accessed | tf_op | source)
XLA Modules:
  0.0 83.6 jit_solution(1324031180346610719)
XLA Ops:
  0.6 0.0 copy-start.5
  0.6 0.0 copy-start.2
  1.3 0.0 copy-done.5
  1.3 0.1 copy.12.wb_ref
  1.4 0.0 copy-done.2
  1.4 0.0 copy-start
  1.4 0.8 %copy-done = bf16[128,256]{1,0:T(8,128)(2,1)S(1)} copy-done((bf16[128,256]{1,0:T(8,128)(2,1)S(1)}, bf16[128,256]{1,0:T(8,128)(2,1)}, u32[]{:S(2)}) %copy-start) | copy-done | bytes 65560
  2.3 0.0 copy-start.1
  2.3 0.8 %copy-done.1 = f32[128,128]{1,0:T(8,128)S(1)} copy-done((f32[128,128]{1,0:T(8,128)S(1)}, f32[128,128]{1,0:T(8,128)}, u32[]{:S(2)}) %copy-start.1) | copy-done | bytes 65560
  3.1 0.0 copy-start.3
  3.1 0.7 copy-done.3
  3.8 0.0 copy-start.4
  3.8 0.7 copy-done.4
  4.5 76.1 %delta_step.1 = (f32[128,128]{1,0:T(8,128)S(1)}, f32[32,128]{1,0:T(8,128)S(1)}, f32[32,128]{1,0:T(8,128)S(1)}, f32[32,128]{1,0:T(8,128)S(1)}, f32[32,1]{1,0:T(8,128)S(1)}) custom-call(bf16[128,256]{1,0:T(8,128)(2,1)S(1)} %copy-done, bf16[32,128]{1,0:T(8,128)(2,1)S(1)} %copy-done.2, bf16[32,128]{1,0:T(8,128)(2,1)S(1)} %copy-done.3, ...), custom_call_target="tpu_custom_call" | custom-call | tf_op jit(solution)/shard_map/delta_step/pallas_call | solution.py:388
  80.6 0.6 copy.13
  81.2 0.6 copy.19
  81.8 0.6 copy.20
  82.4 0.6 copy.21
  83.0 0.6 copy.22
Async XLA Ops:
  0.6 0.7 copy-start.5
  0.6 0.8 copy-start.2
  1.4 0.8 %copy-start = (bf16[128,256]{1,0:T(8,128)(2,1)S(1)}, bf16[128,256]{1,0:T(8,128)(2,1)}, u32[]{:S(2)}) copy-start(bf16[128,256]{1,0:T(8,128)(2,1)} %x_ref.1) | copy-start | bytes 196612
  2.3 0.8 %copy-start.1 = (f32[128,128]{1,0:T(8,128)S(1)}, f32[128,128]{1,0:T(8,128)}, u32[]{:S(2)}) copy-start(f32[128,128]{1,0:T(8,128)} %cot_ref.1) | copy-start | bytes 196612
  3.1 0.7 copy-start.3
  3.8 0.7 copy-start.4

commit v2 on v1

v2 whole, which is shorter than its diff:
```python
import functools
import math

import jax
import jax.numpy as jnp
from jax import lax
from jax.experimental import pallas as pl
from jax.experimental.pallas import tpu as pltpu
from jax.sharding import PartitionSpec as P

MESH = pl.DeviceIdType.MESH
F32 = jnp.float32
BF16 = jnp.bfloat16
NN = (((1,), (0,)), ((), ()))
NT = (((1,), (1,)), ((), ()))


def split(a):
    high = a.astype(BF16)
    return high, (a - high.astype(F32)).astype(BF16)


def mm(a, b, form=NN):
    a_high, a_low = split(a)
    b_high, b_low = split(b)
    return mm1(a_high, b_high, form) + (mm1(a_high, b_low, form) + mm1(a_low, b_high, form))


def mm1(a, b, form=NN):
    return lax.dot_general(a, b, form, preferred_element_type=F32)


def kernel(
    nz, ny, nj,
    x_ref, wq_ref, wk_ref, wv_ref, wb_ref, bias_ref, cot_ref,
    o_out, gq_out, gk_out, gv_out, gb_out,
    o_ref, gq_ref, gk_ref, gv_ref, gb_ref, cotv, wbv, wg, wb1, wb2, xg, xt, xr, ag, bcs, bcr, gbc, ya, ybc, sgs, sgr, ggs, gg, gbs, gbr, ps, pr, pbs, pbr,
    ls, zs, zr, w1s, w1r, w2s, w2r, w3s, w3r, v1s, v1r, v2s, v2r, v3s, v3r, as_, ar, ass, asr, bs, br, y1s, y1r, y2s, y2r, y3s, y3r,
    xs, xrs, ss, sr, gs, grs, hs, hr, ps_, prs, pbs_, pbrs,
):
    h = lax.axis_index("head")
    s = lax.axis_index("seq")
    y = s // nj
    j = lax.rem(s, nj)
    core = lax.rem(j, 2)
    tok, fb = x_ref.shape
    rw, width = wq_ref.shape
    vp = width // nj

    def zdev(d):
        return (lax.rem(h + d + nz, nz), s)

    def yat(d):
        return lax.rem(y + d + ny, ny)

    def ydev(d):
        return (h, yat(d) * nj + j)

    def jat(d):
        return lax.rem(j + d + nj, nj)

    def jdev(d):
        return (h, y * nj + jat(d))

    sib = j + 1 - 2 * core
    sibdev = (h, y * nj + sib)
    sent = []

    def drain():
        for copy in sent:
            copy.wait_send()
        del sent[:]

    def push(src, dst, sems, at, dev):
        copy = pltpu.make_async_remote_copy(
            src_ref=src, dst_ref=dst, send_sem=sems[0].at[at], recv_sem=sems[1].at[at], device_id=dev, device_id_type=MESH
        )
        copy.start()
        sent.append(copy)

    def arrived(dst, sems, at):
        pltpu.make_async_remote_copy(
            src_ref=dst, dst_ref=dst, send_sem=sems[0].at[at], recv_sem=sems[1].at[at], device_id=sibdev, device_id_type=MESH
        ).wait_recv()

    local = [
        pltpu.make_async_copy(x_ref, xg.at[h], ls.at[0]),
        pltpu.make_async_copy(wq_ref, wg.at[j, y, pl.ds(0, rw)], ls.at[1]),
        pltpu.make_async_copy(wk_ref, wg.at[j, y, pl.ds(rw, rw)], ls.at[2]),
        pltpu.make_async_copy(wv_ref, wg.at[j, y, pl.ds(2 * rw, rw)], ls.at[3]),
        pltpu.make_async_copy(cot_ref, cotv, ls.at[4]),
        pltpu.make_async_copy(wb_ref, wbv, ls.at[10]),
    ]
    for copy in local:
        copy.start()

    barrier = pltpu.get_barrier_semaphore()
    for d in (1, nz - 1, 2, nz - 2):
        pl.semaphore_signal(barrier, inc=1, device_id=zdev(d), device_id_type=MESH)
    for d in range(1, ny):
        pl.semaphore_signal(barrier, inc=1, device_id=ydev(d), device_id_type=MESH)
    for d in range(1, nj):
        pl.semaphore_signal(barrier, inc=1, device_id=jdev(d), device_id_type=MESH)

    per = 128 // rw
    lane = lax.broadcasted_iota(jnp.int32, (1, 128), 1)
    for copy in local:
        copy.wait()
    wb_row = jnp.concatenate([wbv[...].astype(F32)] * per, axis=1)
    wb_row = jnp.where(lane // rw == lax.rem(j, per), wb_row, 0.0)
    wb1[y] = jnp.broadcast_to(wb_row, (16, 128)).astype(BF16)

    pl.semaphore_wait(barrier, ny + nj + 2)

    order_y = sorted(range(1, ny), key=lambda d: min(d, ny - d))
    order_j = sorted(range(1, nj), key=lambda d: min(d, nj - d))
    evens = [e for e in order_j if e % 2 == 0]

    for d in order_y:
        push(wg.at[j, y], wg.at[j, y], (w1s, w1r), (d,), ydev(d))
    for n, e in enumerate(evens):
        push(wg.at[j, y], wg.at[j, y], (w2s, w2r), (n, 0), jdev(e))
    for d in (2, nz - 2, 1, nz - 1):
        push(xg.at[h], xg.at[h], (zs, zr), (d,), zdev(d))
    for d in order_y:
        push(wb1.at[y], wb1.at[y], (v1s, v1r), (d,), ydev(d))
    push(wg.at[j, y], wg.at[j, y], (w3s, w3r), (0, 0), sibdev)

    def take_w(d):
        part = wg.at[j, yat(-d)]
        arrived(part, (w1s, w1r), (d,))
        for n, e in enumerate(evens):
            push(part, part, (w2s, w2r), (n, d), jdev(e))
        push(part, part, (w3s, w3r), (0, d), sibdev)

    for d in order_y[:4]:
        take_w(d)
    up, down = lax.rem(h - 2 + nz, nz), lax.rem(h + 2, nz)
    mid = tok // 2
    arrived(xg.at[up], (zs, zr), (2,))
    push(xg.at[up], xg.at[up], (zs, zr), (3,), zdev(1))
    push(xg.at[up, pl.ds(0, mid)], xg.at[up, pl.ds(0, mid)], (zs, zr), (4,), zdev(2))
    arrived(xg.at[down], (zs, zr), (nz - 2,))
    push(xg.at[down], xg.at[down], (zs, zr), (nz - 3,), zdev(-1))
    push(xg.at[down, pl.ds(mid, mid)], xg.at[down, pl.ds(mid, mid)], (zs, zr), (0,), zdev(-2))
    for d in order_y[4:]:
        take_w(d)
    for d in order_y:
        arrived(wb1.at[yat(-d)], (v1s, v1r), (d,))
    turn = lax.broadcasted_iota(jnp.int32, (16, 128), 0)
    col = jnp.zeros((16, 128), F32)
    for b in range(ny):
        col = jnp.where(turn == b, wb1[b].astype(F32), col)
    wb2[j] = col.astype(BF16)
    push(wb2.at[j], wb2.at[j], (v3s, v3r), (0,), sibdev)
    for n, e in enumerate(evens):
        push(wb2.at[j], wb2.at[j], (v2s, v2r), (n,), jdev(e))

    cot = cotv[...]
    cot_t = cot.T

    for d in [0] + order_y:
        for n, e in enumerate(evens):
            part = wg.at[jat(-e), yat(-d)]
            arrived(part, (w2s, w2r), (n, d))
            push(part, part, (w3s, w3r), (n + 1, d), sibdev)
    for n, e in enumerate(evens):
        part = wb2.at[jat(-e)]
        arrived(part, (v2s, v2r), (n,))
        push(part, part, (v3s, v3r), (n + 1,), sibdev)
    for d in (1, nz - 1, 3, nz - 3):
        arrived(xg.at[lax.rem(h - d + nz, nz)], (zs, zr), (d,))
    far = lax.rem(h + 4, nz)
    arrived(xg.at[far, pl.ds(0, mid)], (zs, zr), (4,))
    arrived(xg.at[far, pl.ds(mid, mid)], (zs, zr), (0,))
    for n, e in enumerate([0] + evens):
        part = lax.rem(sib - e + nj, nj)
        for d in [0] + order_y:
            arrived(wg.at[part, yat(-d)], (w3s, w3r), (n, d))
        arrived(wb2.at[part], (v3s, v3r), (n,))

    raw = jnp.zeros((tok, 3 * width), F32)
    lacc = jnp.zeros((tok, 128), F32)
    w_rows = [
        jnp.sum(wb2[g * per:(g + 1) * per].astype(F32), axis=0) for g in range(fb // 128)
    ]
    for b in range(nz):
        xb = xg[b]
        w_b = jnp.concatenate(
            [wg[:, b, m * rw:(m + 1) * rw, :].reshape(fb, width) for m in range(3)], axis=1
        )
        raw = raw + mm1(xb, w_b)
        for g in range(fb // 128):
            w_row = w_rows[g][b:b + 1]
            lacc = lacc + xb[:, g * 128:(g + 1) * 128].astype(F32) * w_row
    logit = jnp.sum(lacc, axis=1, keepdims=True) + bias_ref[0]
    beta = 2.0 * jax.nn.sigmoid(logit)

    def unit(r):
        scale = lax.rsqrt(jnp.mean(r * r, axis=1, keepdims=True) + 1e-06) * (1.0 / math.sqrt(width))
        return r * scale, scale

    q, q_scale = unit(raw[:, :width])
    k, k_scale = unit(raw[:, width:2 * width])
    v = raw[:, 2 * width:]

    ri = lax.broadcasted_iota(jnp.int32, (tok, tok), 0)
    ci = lax.broadcasted_iota(jnp.int32, (tok, tok), 1)
    lower = ri > ci
    upper = ri < ci
    lower_d = ri >= ci
    upper_d = ri <= ci
    eye = jnp.where(ri == ci, 1.0, 0.0).astype(F32)

    gram = mm(k, k, NT)
    low = jnp.where(lower, beta * gram, 0.0)
    t_mat = eye - jnp.where((ri // 2) == (ci // 2), low, 0.0)
    size = 2
    while size < tok:
        level = ((ri // (2 * size)) == (ci // (2 * size))) & ((ri // size) != (ci // size))
        t_mat = t_mat - mm(t_mat, mm(jnp.where(level, low, 0.0), t_mat))
        size *= 2
    k_t = k.T
    w_mat = mm(t_mat, beta * k)
    ag[j] = eye - mm(k_t, w_mat)
    push(ag.at[j], ag.at[j], (ass, asr), (0,), sibdev)
    for n, e in enumerate(evens):
        push(ag.at[j], ag.at[j], (as_, ar), (n,), jdev(e))
    m_mat = jnp.where(lower_d, mm(q, k, NT), 0.0)
    q_eff = q - mm(m_mat, w_mat)
    u_mat = mm(t_mat, beta * v)
    bcs[:, 0] = mm(k_t, u_mat).T.reshape(nj, vp, width)
    bcs[:, 1] = mm(cot_t, q_eff).reshape(nj, vp, width)
    bcr[j] = bcs[j]
    for d in order_j:
        push(bcs.at[jat(d)], bcr.at[j], (bs, br), (d,), jdev(d))

    m_t = jnp.where(upper_d, mm(k, q, NT), 0.0)
    ty = mm(t_mat.T, jnp.concatenate([k, mm(m_t, cot)], axis=1))
    t_k, y_0 = ty[:, :width], ty[:, width:]
    m_u = mm(m_mat, u_mat)
    for b in range(nz):
        xt[:, b * rw:(b + 1) * rw, :] = xg[b].astype(F32).T.astype(BF16).reshape(nj, rw, tok)

    drain()
    for n, e in enumerate(evens):
        part = ag.at[jat(-e)]
        arrived(part, (as_, ar), (n,))
        push(part, part, (ass, asr), (n + 1,), sibdev)
    arrived(ag.at[sib], (ass, asr), (0,))
    for n, e in enumerate(evens):
        arrived(ag.at[lax.rem(sib - e + nj, nj)], (ass, asr), (n + 1,))
    for d in order_j:
        arrived(bcr.at[jat(-d)], (bs, br), (d,))

    pair_p, pair_b, pair_c = [], [], []
    for i in range(0, nj, 2):
        pair_p.append(mm(ag[i + 1], ag[i]))
        pair_b.append(mm(bcr[i, 0], ag[i + 1], NT) + bcr[i + 1, 0])
        pair_c.append(mm(bcr[i + 1, 1], ag[i]) + bcr[i, 1])
    p_mat, b_row, c_row = pair_p[0], pair_b[0], pair_c[-1]
    befores = [None, ag[0], p_mat]
    b_before = [None, bcr[0, 0], b_row]
    c_after = {nj - 2: bcr[nj - 1, 1], nj - 3: c_row}
    for i in range(1, nj // 2):
        back = nj // 2 - 1 - i
        p_mat = mm(pair_p[i], p_mat)
        b_row = mm(b_row, pair_p[i], NT) + pair_b[i]
        c_row = mm(c_row, pair_p[back]) + pair_c[back]
        befores += [None, p_mat]
        b_before += [None, b_row]
        c_after[2 * back - 1] = c_row
    ybc[y] = jnp.zeros((vp, width), F32)
    gbc[0] = b_row
    gbc[1] = c_row
    half = tok // 2
    top, bottom = p_mat[:half].astype(BF16), p_mat[half:].astype(BF16)
    ya[core, y] = jnp.where(core == 0, top, bottom)
    for d in order_y:
        push(ya.at[core, y], ya.at[core, y], (y1s, y1r), (d,), ydev(d))
        side = (y + d) // ny
        push(gbc.at[side], ybc.at[y], (y2s, y2r), (d,), ydev(d))
    for d in order_j:
        xr_dst = xr.at[j]
        push(xt.at[jat(d)], xr_dst, (xs, xrs), (d,), jdev(d))
    xr[j] = xt[j]

    afters = {nj - 2: ag[nj - 1], nj - 3: pair_p[-1]}
    for i in range(nj // 2 - 2, -1, -1):
        afters[2 * i - 1] = mm(afters[2 * i + 1], pair_p[i])
        afters[2 * i] = mm(afters[2 * i + 1], ag[2 * i + 1])
        c_after[2 * i] = mm(c_after[2 * i + 1], ag[2 * i + 1]) + bcr[2 * i + 1, 1]
        m = nj - 2 - 2 * i
        befores[m + 1] = mm(ag[m], befores[m])
        b_before[m + 1] = mm(b_before[m], ag[m], NT) + bcr[m, 0]
    drain()
    for d in order_y:
        arrived(ya.at[core, yat(-d)], (y1s, y1r), (d,))
    push(ya.at[core], ya.at[core], (y3s, y3r), (0,), sibdev)
    for d in order_y:
        arrived(ybc.at[yat(-d)], (y2s, y2r), (d,))
    arrived(ya.at[1 - core], (y3s, y3r), (0,))

    def full(t):
        return jnp.concatenate([ya[0, t], ya[1, t]], axis=0).astype(F32)

    s_g = jnp.zeros((vp, width), F32)
    g_g = jnp.zeros((vp, width), F32)
    for t in range(ny - 1):
        s_g = jnp.where(t < y, mm(s_g, full(t), NT) + ybc[t], s_g)
        u = ny - 1 - t
        g_g = jnp.where(u > y, mm(g_g, full(u)) + ybc[u], g_g)

    sgs[0, 0] = s_g
    sgs[nj - 1, 1] = g_g
    for i in range(1, nj):
        sgs[i, 0] = mm(s_g, befores[i], NT) + b_before[i]
    for i in range(nj - 1):
        sgs[i, 1] = mm(g_g, afters[i]) + c_after[i]
    for d in order_j:
        push(sgs.at[jat(d)], sgr.at[j], (ss, sr), (d,), jdev(d))
    sgr[j] = sgs[j]
    drain()
    for d in order_j:
        arrived(sgr.at[jat(-d)], (ss, sr), (d,))

    state = sgr[:, 0].reshape(width, width)
    grad = sgr[:, 1].reshape(width, width)
    y_mat = y_0 + mm(t_k, grad, NT)
    b_y = beta * y_mat
    ggs[2] = b_y.astype(BF16)

    def share(src, dst, m):
        push(src, dst, (hs, hr), (m, 0), sibdev)
        for n, e in enumerate(evens):
            push(src, dst, (gs, grs), (m, n), jdev(e))

    def shared(at, m):
        for n, e in enumerate(evens):
            part = at(jat(-e))
            arrived(part, (gs, grs), (m, n))
            push(part, part, (hs, hr), (m, n + 1), sibdev)

    def collected(at, m):
        for n, e in enumerate([0] + evens):
            arrived(at(lax.rem(sib - e + nj, nj)), (hs, hr), (m, n))

    gg[j, 2] = ggs[2]
    share(ggs.at[2], gg.at[j, 2], 2)
    fresh = u_mat - mm(w_mat, state, NT)
    o_ref[...] = mm(q_eff, state, NT) + m_u
    stores = [pltpu.make_async_copy(o_ref, o_out, ls.at[5])]
    stores[0].start()
    d_m = jnp.where(lower_d, mm(cot, fresh, NT), 0.0)
    d_q = mm(cot, state) + mm(d_m, k)
    ggs[0] = (q_scale * (d_q - q * jnp.sum(d_q * q, axis=1, keepdims=True))).astype(BF16)
    gg[j, 0] = ggs[0]
    share(ggs.at[0], gg.at[j, 0], 0)
    rest = v - mm(k, state, NT)
    d_mt = jnp.where(upper_d, mm(fresh, cot, NT), 0.0)
    yd = jnp.where(lower, mm(y_mat, fresh, NT), 0.0)
    both = beta * yd + jnp.where(upper, mm(fresh, b_y, NT), 0.0)
    d_k = mm(fresh, grad) - mm(b_y, state) + mm(d_mt, q) - mm(both, k)
    ggs[1] = (k_scale * (d_k - k * jnp.sum(d_k * k, axis=1, keepdims=True))).astype(BF16)
    gg[j, 1] = ggs[1]
    share(ggs.at[1], gg.at[j, 1], 1)
    d_beta = jnp.sum(y_mat * rest - yd * gram, axis=1, keepdims=True)
    d_logit = d_beta * beta * (1.0 - 0.5 * beta)
    dl_row = jnp.sum(eye * d_logit, axis=0, keepdims=True)
    gbs[...] = jnp.broadcast_to(dl_row, (16, tok)).astype(BF16)
    gbr[j] = gbs[...]
    share(gbs, gbr.at[j], 3)

    for d in order_j:
        arrived(xr.at[jat(-d)], (xs, xrs), (d,))
    x_t = jnp.concatenate([xr[i] for i in range(nj)], axis=1)

    outs = {0: gq_ref, 1: gk_ref, 2: gv_ref}
    places = [
        lambda i: gg.at[i, 0],
        lambda i: gg.at[i, 1],
        lambda i: gg.at[i, 2],
        lambda i: gbr.at[i],
    ]
    def spread(m):
        collected(places[m], m)
        part = mm1(x_t, gg[:, m].reshape(nj * tok, width)).reshape(ny, rw, width)
        pr[m, y] = jnp.zeros((rw, width), BF16)
        ps[m] = part.astype(BF16)
        for d in order_y:
            push(ps.at[m, yat(d)], pr.at[m, y], (ps_, prs), (m, d), ydev(d))
        own = part[0]
        for t in range(1, ny):
            own = jnp.where(t == y, part[t], own)
        outs[m][...] = own

    for m in (2, 0, 1, 3):
        shared(places[m], m)
    for m in (2, 0, 1):
        spread(m)
    collected(places[3], 3)
    pb = mm1(jnp.concatenate([gbr[i] for i in range(nj)], axis=1), x_t, NT)
    for g in range(fb // 128):
        pbs[g] = pb[:8, g * 128:(g + 1) * 128]
    for d in order_y:
        push(pbs.at[yat(d) * rw // 128], pbr.at[y], (pbs_, pbrs), (d,), ydev(d))
    pbr[y] = pbs[y * rw // 128]

    def store(src, dst, at):
        stores.append(pltpu.make_async_copy(src, dst, ls.at[at]))
        stores[-1].start()

    out_refs = {0: gq_out, 1: gk_out, 2: gv_out}
    for m in (2, 0, 1):
        for d in order_y:
            arrived(pr.at[m, yat(-d)], (ps_, prs), (m, d))
        outs[m][...] += jnp.sum(pr[m].astype(F32), axis=0)
        store(outs[m], out_refs[m], 6 + m)
    for d in order_y:
        arrived(pbr.at[yat(-d)], (pbs_, pbrs), (d,))
    pb_row = jnp.sum(pbr[...], axis=0)[:1]
    gb_row = jnp.zeros((1, rw), F32)
    for g in range(per):
        gb_row = jnp.where(lax.rem(y, per) == g, pb_row[:, g * rw:(g + 1) * rw], gb_row)
    gb_ref[...] = gb_row
    store(gb_ref, gb_out, 9)

    drain()
    for copy in stores:
        copy.wait()


def write_out(o_in, gq_in, gk_in, gv_in, gb_in, o_out, gq_out, gk_out, gv_out, gb_out, sems):
    pairs = [(o_in, o_out), (gq_in, gq_out), (gk_in, gk_out), (gv_in, gv_out), (gb_in, gb_out)]
    copies = [pltpu.make_async_copy(pairs[i][0], pairs[i][1], sems.at[i]) for i in range(5)]
    for copy in copies:
        copy.start()
    for copy in copies:
        copy.wait()


def per_device(mesh, *args):
    inputs, w_query, w_key, w_value, w_beta, beta_bias, cotangent = args
    nz = mesh.shape["head"]
    ny = nz
    nj = mesh.shape["seq"] // ny
    tok, fb = inputs.shape
    rw, width = w_query.shape
    vp = width // nj
    ne = nj // 2
    vmem = pl.BlockSpec(memory_space=pltpu.VMEM)
    hbm = pl.BlockSpec(memory_space=pl.ANY)
    dma = pltpu.SemaphoreType.DMA
    scratch = [
        pltpu.VMEM((tok, width), F32),
        pltpu.VMEM((rw, width), F32),
        pltpu.VMEM((rw, width), F32),
        pltpu.VMEM((rw, width), F32),
        pltpu.VMEM((1, rw), F32),
        pltpu.VMEM((tok, width), F32),
        pltpu.VMEM((1, rw), BF16),
        pltpu.VMEM((nj, ny, 3 * rw, width), BF16),
        pltpu.VMEM((ny, 16, 128), BF16),
        pltpu.VMEM((nj, 16, 128), BF16),
        pltpu.VMEM((nz, tok, fb), BF16),
        pltpu.VMEM((nj, nz * rw, tok), BF16),
        pltpu.VMEM((nj, nz * rw, tok), BF16),
        pltpu.VMEM((nj, width, width), F32),
        pltpu.VMEM((nj, 2, vp, width), F32),
        pltpu.VMEM((nj, 2, vp, width), F32),
        pltpu.VMEM((2, vp, width), F32),
        pltpu.VMEM((2, ny, width // 2, width), BF16),
        pltpu.VMEM((ny, vp, width), F32),
        pltpu.VMEM((nj, 2, vp, width), F32),
        pltpu.VMEM((nj, 2, vp, width), F32),
        pltpu.VMEM((3, tok, width), BF16),
        pltpu.VMEM((nj, 3, tok, width), BF16),
        pltpu.VMEM((16, tok), BF16),
        pltpu.VMEM((nj, 16, tok), BF16),
        pltpu.VMEM((3, ny, rw, width), BF16),
        pltpu.VMEM((3, ny, rw, width), BF16),
        pltpu.VMEM((fb // 128, 8, 128), F32),
        pltpu.VMEM((ny, 8, 128), F32),
        dma((11,)),
        dma((nz,)), dma((nz,)),
        dma((ny,)), dma((ny,)),
        dma((ne, ny)), dma((ne, ny)),
        dma((ne, ny)), dma((ne, ny)),
        dma((ny,)), dma((ny,)),
        dma((ne,)), dma((ne,)),
        dma((ne,)), dma((ne,)),
        dma((ne,)), dma((ne,)),
        dma((ne,)), dma((ne,)),
        dma((nj,)), dma((nj,)),
        dma((ny,)), dma((ny,)),
        dma((ny,)), dma((ny,)),
        dma((1,)), dma((1,)),
        dma((nj,)), dma((nj,)),
        dma((nj,)), dma((nj,)),
        dma((4, ne)), dma((4, ne)),
        dma((4, ne)), dma((4, ne)),
        dma((3, ny)), dma((3, ny)),
        dma((ny,)), dma((ny,)),
    ]
    results = pl.pallas_call(
        functools.partial(kernel, nz, ny, nj),
        out_shape=(
            jax.ShapeDtypeStruct((tok, width), F32),
            jax.ShapeDtypeStruct((rw, width), F32),
            jax.ShapeDtypeStruct((rw, width), F32),
            jax.ShapeDtypeStruct((rw, width), F32),
            jax.ShapeDtypeStruct((1, rw), F32),
        ),
        in_specs=[hbm, hbm, hbm, hbm, hbm, pl.BlockSpec(memory_space=pltpu.SMEM), hbm],
        out_specs=(hbm,) * 5,
        scratch_shapes=scratch,
        compiler_params=pltpu.CompilerParams(
            collective_id=0, has_side_effects=True, vmem_limit_bytes=60 * 1024 * 1024
        ),
        name="delta_step",
    )(inputs, w_query, w_key, w_value, w_beta.reshape(1, rw), beta_bias, cotangent)
    results = pl.pallas_call(
        write_out,
        out_shape=[jax.ShapeDtypeStruct(r.shape, F32) for r in results],
        in_specs=[vmem] * 5,
        out_specs=[hbm] * 5,
        scratch_shapes=[dma((5,))],
        name="write_out",
    )(*results)
    return (results[0], results[1], results[2], results[3], results[4].reshape(rw, 1))


def solution(mesh):
    return jax.shard_map(
        functools.partial(per_device, mesh),
        mesh=mesh,
        in_specs=(P("seq", "head"),) * 5 + (P("head"), P("seq", "head")),
        out_specs=(P("seq", "head"),) * 5,
        check_vma=False,
    )
```

time: 84 us -> 74.6 us (0.89)
  local copies, waits for them, and re-layouts: 6.21 us -> 0 us
  Pallas kernels: 76.1 us -> 72.9 us
    unnamed x17 -> x0, local copies, waits for them, and re-layouts: 5.63 us -> none
    pallas_call x1, Pallas kernels: 76.1 us -> 71.3 us  [per_device(): pl.pallas_call(functools.partial(kernel, nz, ny, nj), out_shape=(jax.Shap...]
    pallas_call x0 -> x1, Pallas kernels: none -> 1.56 us  [per_device(): pl.pallas_call(write_out, out_shape=[jax.ShapeDtypeStruct(r.shape, F32) f...]
where the time goes in v2:
time: 74.6 us; the launch traced here: 74.1 us
  Pallas kernels  72.9 us (98%)
  between operations  1.29 us (2%)
    pallas_call x1, Pallas kernels, per_device(): pl.pallas_call(functools.partial(kernel, nz, ny, nj), out_shape=(jax.Shap...  71.3 us
    pallas_call x1, Pallas kernels, per_device(): pl.pallas_call(write_out, out_shape=[jax.ShapeDtypeStruct(r.shape, F32) f...  1.56 us

profile of v2, /device:TPU:1, one launch (start us, length us, event | category | flops | bytes accessed | tf_op | source)
XLA Modules:
  0.0 74.1 jit_solution(384649962095948416)
XLA Ops:
  1.3 71.3 %delta_step.1 = (f32[128,128]{1,0:T(8,128)}, f32[32,128]{1,0:T(8,128)}, f32[32,128]{1,0:T(8,128)}, f32[32,128]{1,0:T(8,128)}, f32[1,32]{1,0:T(1,128)}) custom-call(bf16[128,256]{1,0:T(8,128)(2,1)} %x_ref.1, bf16[32,128]{1,0:T(8,128)(2,1)} %wq_ref.1, bf16[32,128]{1,0:T(8,128)(2,1)} %wk_ref.1, bf16[32,128]{1,0:T(8,128)(2,1)} %wv_ref.1, bf16[1,32]{1,0:T(2,128)(2,1)} %bitcast.2, ...), custom_call_target="tpu_custom_call" | custom-call | tf_op jit(solution)/shard_map/delta_step/pallas_call | solution.py:505
  72.6 1.6 %write_out.1 = (f32[128,128]{1,0:T(8,128)}, f32[32,128]{1,0:T(8,128)}, f32[32,128]{1,0:T(8,128)}, f32[32,128]{1,0:T(8,128)}, f32[1,32]{1,0:T(1,128)}) custom-call(f32[128,128]{1,0:T(8,128)} %get-tuple-element.15.o_in, f32[32,128]{1,0:T(8,128)} %get-tuple-element.16.gq_in, f32[32,128]{1,0:T(8,128)} %get-tuple-element.17.gk_in, ...), custom_call_target="tpu_custom_call" | custom-call | tf_op jit(solution)/shard_map/write_out/pallas_call | solution.py:522

commit v3 on v2

--- a/solution.py
+++ b/solution.py
@@ -34,8 +34,8 @@
     nz, ny, nj,
     x_ref, wq_ref, wk_ref, wv_ref, wb_ref, bias_ref, cot_ref,
     o_out, gq_out, gk_out, gv_out, gb_out,
-    o_ref, gq_ref, gk_ref, gv_ref, gb_ref, cotv, wbv, wg, wb1, wb2, xg, xt, xr, ag, bcs, bcr, gbc, ya, ybc, sgs, sgr, ggs, gg, gbs, gbr, ps, pr, pbs, pbr,
-    ls, zs, zr, w1s, w1r, w2s, w2r, w3s, w3r, v1s, v1r, v2s, v2r, v3s, v3r, as_, ar, ass, asr, bs, br, y1s, y1r, y2s, y2r, y3s, y3r,
+    o_ref, gq_ref, gk_ref, gv_ref, gb_ref, cotv, wbv, wg, wq, wb1, wb2, xg, xt, xr, ag, bcs, bcr, gbc, ya, ybc, sgs, sgr, ggs, gg, gbs, gbr, ps, pr, pbs, pbr,
+    ls, zs, zr, w1s, w1r, w2s, w2r, w3s, w3r, q1s, q1r, q2s, q2r, q3s, q3r, v1s, v1r, v2s, v2r, v3s, v3r, as_, ar, ass, asr, bs, br, y1s, y1r, y2s, y2r, y3s, y3r,
     xs, xrs, ss, sr, gs, grs, hs, hr, ps_, prs, pbs_, pbrs,
 ):
     h = lax.axis_index("head")
@@ -85,9 +85,9 @@
 
     local = [
         pltpu.make_async_copy(x_ref, xg.at[h], ls.at[0]),
-        pltpu.make_async_copy(wq_ref, wg.at[j, y, pl.ds(0, rw)], ls.at[1]),
-        pltpu.make_async_copy(wk_ref, wg.at[j, y, pl.ds(rw, rw)], ls.at[2]),
-        pltpu.make_async_copy(wv_ref, wg.at[j, y, pl.ds(2 * rw, rw)], ls.at[3]),
+        pltpu.make_async_copy(wq_ref, wq.at[j, y, pl.ds(0, rw)], ls.at[1]),
+        pltpu.make_async_copy(wk_ref, wg.at[j, y], ls.at[2]),
+        pltpu.make_async_copy(wv_ref, wq.at[j, y, pl.ds(rw, rw)], ls.at[3]),
         pltpu.make_async_copy(cot_ref, cotv, ls.at[4]),
         pltpu.make_async_copy(wb_ref, wbv, ls.at[10]),
     ]
@@ -95,8 +95,12 @@
         copy.start()
 
     barrier = pltpu.get_barrier_semaphore()
-    for d in (1, nz - 1, 2, nz - 2):
+    for d in (-1, -2):
         pl.semaphore_signal(barrier, inc=1, device_id=zdev(d), device_id_type=MESH)
+    for d in (1, 2):
+        @pl.when(h + d < nz)
+        def _():
+            pl.semaphore_signal(barrier, inc=1, device_id=zdev(d), device_id_type=MESH)
     for d in range(1, ny):
         pl.semaphore_signal(barrier, inc=1, device_id=ydev(d), device_id_type=MESH)
     for d in range(1, nj):
@@ -110,7 +114,7 @@
     wb_row = jnp.where(lane // rw == lax.rem(j, per), wb_row, 0.0)
     wb1[y] = jnp.broadcast_to(wb_row, (16, 128)).astype(BF16)
 
-    pl.semaphore_wait(barrier, ny + nj + 2)
+    pl.semaphore_wait(barrier, ny + nj + 2 - jnp.maximum(2 - h, 0))
 
     order_y = sorted(range(1, ny), key=lambda d: min(d, ny - d))
     order_j = sorted(range(1, nj), key=lambda d: min(d, nj - d))
@@ -120,10 +124,56 @@
         push(wg.at[j, y], wg.at[j, y], (w1s, w1r), (d,), ydev(d))
     for n, e in enumerate(evens):
         push(wg.at[j, y], wg.at[j, y], (w2s, w2r), (n, 0), jdev(e))
-    for d in (2, nz - 2, 1, nz - 1):
-        push(xg.at[h], xg.at[h], (zs, zr), (d,), zdev(d))
+    up, down = lax.rem(h - 2 + nz, nz), lax.rem(h + 2, nz)
+    mid = tok // 2
+
+    def send(src, at, d):
+        copy = pltpu.make_async_remote_copy(
+            src_ref=src, dst_ref=src, send_sem=zs.at[at], recv_sem=zr.at[at],
+            device_id=zdev(d), device_id_type=MESH,
+        )
+        return copy
+
+    def z_copies():
+        return {
+            2: send(xg.at[h], 2, 2),
+            1: send(xg.at[h], 1, 1),
+            -2: send(xg.at[h], nz - 2, -2),
+            -1: send(xg.at[h], nz - 1, -1),
+            3: send(xg.at[up], 3, 1),
+            4: send(xg.at[up, pl.ds(0, mid)], 4, 2),
+            -3: send(xg.at[down], nz - 3, -1),
+            -4: send(xg.at[down, pl.ds(mid, mid)], 0, -2),
+        }
+
+    def got(d):
+        return send(xg.at[lax.rem(h - d + nz, nz)], d % nz, 1).wait_recv
+
+    z_copies()[2].start()
+    z_copies()[1].start()
+
+    @pl.when(h >= 2)
+    def _():
+        z_copies()[-2].start()
+
+    @pl.when(h >= 1)
+    def _():
+        z_copies()[-1].start()
+
+    def pass_up():
+        got(2)()
+        z_copies()[3].start()
+        z_copies()[4].start()
+
+    def pass_down():
+        got(1)()
+        got(-2)()
+        z_copies()[-3].start()
+        z_copies()[-4].start()
     for d in order_y:
         push(wb1.at[y], wb1.at[y], (v1s, v1r), (d,), ydev(d))
+    for d in order_y:
+        push(wq.at[j, y], wq.at[j, y], (q1s, q1r), (d,), ydev(d))
     push(wg.at[j, y], wg.at[j, y], (w3s, w3r), (0, 0), sibdev)
 
     def take_w(d):
@@ -135,14 +185,11 @@
 
     for d in order_y[:4]:
         take_w(d)
-    up, down = lax.rem(h - 2 + nz, nz), lax.rem(h + 2, nz)
-    mid = tok // 2
-    arrived(xg.at[up], (zs, zr), (2,))
-    push(xg.at[up], xg.at[up], (zs, zr), (3,), zdev(1))
-    push(xg.at[up, pl.ds(0, mid)], xg.at[up, pl.ds(0, mid)], (zs, zr), (4,), zdev(2))
-    arrived(xg.at[down], (zs, zr), (nz - 2,))
-    push(xg.at[down], xg.at[down], (zs, zr), (nz - 3,), zdev(-1))
-    push(xg.at[down, pl.ds(mid, mid)], xg.at[down, pl.ds(mid, mid)], (zs, zr), (0,), zdev(-2))
+    @pl.when(h >= 2)
+    def _():
+        pass_up()
+        pass_down()
+
     for d in order_y[4:]:
         take_w(d)
     for d in order_y:
@@ -156,6 +203,29 @@
     for n, e in enumerate(evens):
         push(wb2.at[j], wb2.at[j], (v2s, v2r), (n,), jdev(e))
 
+    for d in order_y:
+        arrived(wq.at[j, yat(-d)], (q1s, q1r), (d,))
+    for n, e in enumerate(evens):
+        push(wq.at[j], wq.at[j], (q2s, q2r), (n,), jdev(e))
+    push(wq.at[j], wq.at[j], (q3s, q3r), (0,), sibdev)
+
+    @pl.when(h < 2)
+    def _():
+        pass_up()
+        z_copies()[-2].start()
+
+        @pl.when(h < 1)
+        def _():
+            got(1)()
+            z_copies()[-1].start()
+
+        @pl.when(h >= 1)
+        def _():
+            got(1)()
+        got(-2)()
+        z_copies()[-3].start()
+        z_copies()[-4].start()
+
     cot = cotv[...]
     cot_t = cot.T
 
@@ -168,31 +238,27 @@
         part = wb2.at[jat(-e)]
         arrived(part, (v2s, v2r), (n,))
         push(part, part, (v3s, v3r), (n + 1,), sibdev)
-    for d in (1, nz - 1, 3, nz - 3):
-        arrived(xg.at[lax.rem(h - d + nz, nz)], (zs, zr), (d,))
+    for d in (-1, 3, -3):
+        got(d)()
     far = lax.rem(h + 4, nz)
-    arrived(xg.at[far, pl.ds(0, mid)], (zs, zr), (4,))
-    arrived(xg.at[far, pl.ds(mid, mid)], (zs, zr), (0,))
+    send(xg.at[far, pl.ds(0, mid)], 4, 2).wait_recv()
+    send(xg.at[far, pl.ds(mid, mid)], 0, -2).wait_recv()
     for n, e in enumerate([0] + evens):
         part = lax.rem(sib - e + nj, nj)
         for d in [0] + order_y:
             arrived(wg.at[part, yat(-d)], (w3s, w3r), (n, d))
         arrived(wb2.at[part], (v3s, v3r), (n,))
 
-    raw = jnp.zeros((tok, 3 * width), F32)
+    raw = jnp.zeros((tok, width), F32)
     lacc = jnp.zeros((tok, 128), F32)
     w_rows = [
         jnp.sum(wb2[g * per:(g + 1) * per].astype(F32), axis=0) for g in range(fb // 128)
     ]
     for b in range(nz):
         xb = xg[b]
-        w_b = jnp.concatenate(
-            [wg[:, b, m * rw:(m + 1) * rw, :].reshape(fb, width) for m in range(3)], axis=1
-        )
-        raw = raw + mm1(xb, w_b)
+        raw = raw + mm1(xb, wg[:, b].reshape(fb, width))
         for g in range(fb // 128):
-            w_row = w_rows[g][b:b + 1]
-            lacc = lacc + xb[:, g * 128:(g + 1) * 128].astype(F32) * w_row
+            lacc = lacc + xb[:, g * 128:(g + 1) * 128].astype(F32) * w_rows[g][b:b + 1]
     logit = jnp.sum(lacc, axis=1, keepdims=True) + bias_ref[0]
     beta = 2.0 * jax.nn.sigmoid(logit)
 
@@ -200,10 +266,7 @@
         scale = lax.rsqrt(jnp.mean(r * r, axis=1, keepdims=True) + 1e-06) * (1.0 / math.sqrt(width))
         return r * scale, scale
 
-    q, q_scale = unit(raw[:, :width])
-    k, k_scale = unit(raw[:, width:2 * width])
-    v = raw[:, 2 * width:]
-
+    k, k_scale = unit(raw)
     ri = lax.broadcasted_iota(jnp.int32, (tok, tok), 0)
     ci = lax.broadcasted_iota(jnp.int32, (tok, tok), 1)
     lower = ri > ci
@@ -214,18 +277,43 @@
 
     gram = mm(k, k, NT)
     low = jnp.where(lower, beta * gram, 0.0)
-    t_mat = eye - jnp.where((ri // 2) == (ci // 2), low, 0.0)
-    size = 2
+    first = jnp.where((ri // 4) == (ci // 4), low, 0.0)
+    t_mat = eye - first
+    t_mat = t_mat + mm(t_mat, mm(first, first))
+    size = 4
     while size < tok:
-        level = ((ri // (2 * size)) == (ci // (2 * size))) & ((ri // size) != (ci // size))
-        t_mat = t_mat - mm(t_mat, mm(jnp.where(level, low, 0.0), t_mat))
-        size *= 2
+        if 2 * size == tok:
+            for n, e in enumerate(evens):
+                part = wq.at[jat(-e)]
+                arrived(part, (q2s, q2r), (n,))
+                push(part, part, (q3s, q3r), (n + 1,), sibdev)
+        wide = min(4 * size, tok)
+        level = ((ri // wide) == (ci // wide)) & ((ri // size) != (ci // size))
+        step = mm(jnp.where(level, low, 0.0), t_mat)
+        if wide == 4 * size:
+            square = mm(step, step)
+            t_mat = t_mat - mm(t_mat, step)
+            t_mat = t_mat + mm(t_mat, square)
+        else:
+            t_mat = t_mat - mm(t_mat, step)
+        size = wide
     k_t = k.T
     w_mat = mm(t_mat, beta * k)
     ag[j] = eye - mm(k_t, w_mat)
     push(ag.at[j], ag.at[j], (ass, asr), (0,), sibdev)
     for n, e in enumerate(evens):
         push(ag.at[j], ag.at[j], (as_, ar), (n,), jdev(e))
+
+    for n, e in enumerate([0] + evens):
+        arrived(wq.at[lax.rem(sib - e + nj, nj)], (q3s, q3r), (n,))
+    raw = jnp.zeros((tok, 2 * width), F32)
+    for b in range(nz):
+        w_b = jnp.concatenate(
+            [wq[:, b, m * rw:(m + 1) * rw, :].reshape(fb, width) for m in range(2)], axis=1
+        )
+        raw = raw + mm1(xg[b], w_b)
+    q, q_scale = unit(raw[:, :width])
+    v = raw[:, width:]
     m_mat = jnp.where(lower_d, mm(q, k, NT), 0.0)
     q_eff = q - mm(m_mat, w_mat)
     u_mat = mm(t_mat, beta * v)
@@ -243,6 +331,8 @@
         xt[:, b * rw:(b + 1) * rw, :] = xg[b].astype(F32).T.astype(BF16).reshape(nj, rw, tok)
 
     drain()
+    for copy in z_copies().values():
+        copy.wait_send()
     for n, e in enumerate(evens):
         part = ag.at[jat(-e)]
         arrived(part, (as_, ar), (n,))
@@ -459,7 +549,8 @@
         pltpu.VMEM((1, rw), F32),
         pltpu.VMEM((tok, width), F32),
         pltpu.VMEM((1, rw), BF16),
-        pltpu.VMEM((nj, ny, 3 * rw, width), BF16),
+        pltpu.VMEM((nj, ny, rw, width), BF16),
+        pltpu.VMEM((nj, ny, 2 * rw, width), BF16),
         pltpu.VMEM((ny, 16, 128), BF16),
         pltpu.VMEM((nj, 16, 128), BF16),
         pltpu.VMEM((nz, tok, fb), BF16),
@@ -486,6 +577,9 @@
         dma((ny,)), dma((ny,)),
         dma((ne, ny)), dma((ne, ny)),
         dma((ne, ny)), dma((ne, ny)),
+        dma((ny,)), dma((ny,)),
+        dma((ne,)), dma((ne,)),
+        dma((ne,)), dma((ne,)),
         dma((ny,)), dma((ny,)),
         dma((ne,)), dma((ne,)),
         dma((ne,)), dma((ne,)),

time: 74.6 us -> 74.2 us (level)
  Pallas kernels: 72.9 us -> 72 us
    pallas_call x1, Pallas kernels: 71.3 us -> 70.4 us  [per_device(): pl.pallas_call(functools.partial(kernel, nz, ny, nj), out_shape=(jax.Shap...]
where the time goes in v3:
time: 74.2 us; the launch traced here: 73.3 us
  Pallas kernels  72 us (97%)
  between operations  1.29 us (2%)
    pallas_call x1, Pallas kernels, per_device(): pl.pallas_call(functools.partial(kernel, nz, ny, nj), out_shape=(jax.Shap...  70.4 us
    pallas_call x1, Pallas kernels, per_device(): pl.pallas_call(write_out, out_shape=[jax.ShapeDtypeStruct(r.shape, F32) f...  1.56 us

profile of v3, /device:TPU:1, one launch (start us, length us, event | category | flops | bytes accessed | tf_op | source)
XLA Modules:
  0.0 73.3 jit_solution(14412677379412308397)
XLA Ops:
  1.3 70.4 %delta_step.1 = (f32[128,128]{1,0:T(8,128)}, f32[32,128]{1,0:T(8,128)}, f32[32,128]{1,0:T(8,128)}, f32[32,128]{1,0:T(8,128)}, f32[1,32]{1,0:T(1,128)}) custom-call(bf16[128,256]{1,0:T(8,128)(2,1)} %x_ref.1, bf16[32,128]{1,0:T(8,128)(2,1)} %wq_ref.1, bf16[32,128]{1,0:T(8,128)(2,1)} %wk_ref.1, bf16[32,128]{1,0:T(8,128)(2,1)} %wv_ref.1, bf16[1,32]{1,0:T(2,128)(2,1)} %bitcast.2, ...), custom_call_target="tpu_custom_call" | custom-call | tf_op jit(solution)/shard_map/delta_step/pallas_call | solution.py:599
  71.7 1.6 %write_out.1 = (f32[128,128]{1,0:T(8,128)}, f32[32,128]{1,0:T(8,128)}, f32[32,128]{1,0:T(8,128)}, f32[32,128]{1,0:T(8,128)}, f32[1,32]{1,0:T(1,128)}) custom-call(f32[128,128]{1,0:T(8,128)} %get-tuple-element.15.o_in, f32[32,128]{1,0:T(8,128)} %get-tuple-element.16.gq_in, f32[32,128]{1,0:T(8,128)} %get-tuple-element.17.gk_in, ...), custom_call_target="tpu_custom_call" | custom-call | tf_op jit(solution)/shard_map/write_out/pallas_call | solution.py:616

commit v4 on v3

--- a/solution.py
+++ b/solution.py
@@ -119,6 +119,8 @@
     order_y = sorted(range(1, ny), key=lambda d: min(d, ny - d))
     order_j = sorted(range(1, nj), key=lambda d: min(d, nj - d))
     evens = [e for e in order_j if e % 2 == 0]
+    far_y, far_j = order_y[::-1], order_j[::-1]
+    far_evens = [(n, e) for n, e in enumerate(evens)][::-1]
 
     for d in order_y:
         push(wg.at[j, y], wg.at[j, y], (w1s, w1r), (d,), ydev(d))
@@ -301,7 +303,7 @@
     w_mat = mm(t_mat, beta * k)
     ag[j] = eye - mm(k_t, w_mat)
     push(ag.at[j], ag.at[j], (ass, asr), (0,), sibdev)
-    for n, e in enumerate(evens):
+    for n, e in far_evens:
         push(ag.at[j], ag.at[j], (as_, ar), (n,), jdev(e))
 
     for n, e in enumerate([0] + evens):
@@ -320,7 +322,7 @@
     bcs[:, 0] = mm(k_t, u_mat).T.reshape(nj, vp, width)
     bcs[:, 1] = mm(cot_t, q_eff).reshape(nj, vp, width)
     bcr[j] = bcs[j]
-    for d in order_j:
+    for d in far_j:
         push(bcs.at[jat(d)], bcr.at[j], (bs, br), (d,), jdev(d))
 
     m_t = jnp.where(upper_d, mm(k, q, NT), 0.0)
@@ -366,7 +368,7 @@
     half = tok // 2
     top, bottom = p_mat[:half].astype(BF16), p_mat[half:].astype(BF16)
     ya[core, y] = jnp.where(core == 0, top, bottom)
-    for d in order_y:
+    for d in far_y:
         push(ya.at[core, y], ya.at[core, y], (y1s, y1r), (d,), ydev(d))
         side = (y + d) // ny
         push(gbc.at[side], ybc.at[y], (y2s, y2r), (d,), ydev(d))
@@ -407,7 +409,7 @@
         sgs[i, 0] = mm(s_g, befores[i], NT) + b_before[i]
     for i in range(nj - 1):
         sgs[i, 1] = mm(g_g, afters[i]) + c_after[i]
-    for d in order_j:
+    for d in far_j:
         push(sgs.at[jat(d)], sgr.at[j], (ss, sr), (d,), jdev(d))
     sgr[j] = sgs[j]
     drain()
@@ -421,9 +423,9 @@
     ggs[2] = b_y.astype(BF16)
 
     def share(src, dst, m):
+        for n, e in far_evens:
+            push(src, dst, (gs, grs), (m, n), jdev(e))
         push(src, dst, (hs, hr), (m, 0), sibdev)
-        for n, e in enumerate(evens):
-            push(src, dst, (gs, grs), (m, n), jdev(e))
 
     def shared(at, m):
         for n, e in enumerate(evens):
@@ -477,7 +479,7 @@
         part = mm1(x_t, gg[:, m].reshape(nj * tok, width)).reshape(ny, rw, width)
         pr[m, y] = jnp.zeros((rw, width), BF16)
         ps[m] = part.astype(BF16)
-        for d in order_y:
+        for d in far_y:
             push(ps.at[m, yat(d)], pr.at[m, y], (ps_, prs), (m, d), ydev(d))
         own = part[0]
         for t in range(1, ny):
@@ -492,7 +494,7 @@
     pb = mm1(jnp.concatenate([gbr[i] for i in range(nj)], axis=1), x_t, NT)
     for g in range(fb // 128):
         pbs[g] = pb[:8, g * 128:(g + 1) * 128]
-    for d in order_y:
+    for d in far_y:
         push(pbs.at[yat(d) * rw // 128], pbr.at[y], (pbs_, pbrs), (d,), ydev(d))
     pbr[y] = pbs[y * rw // 128]
 

time: 74.2 us -> 71.8 us (0.968)
  Pallas kernels: 72 us -> 69.3 us
    pallas_call x1, Pallas kernels: 70.4 us -> 67.7 us  [per_device(): pl.pallas_call(functools.partial(kernel, nz, ny, nj), out_shape=(jax.Shap...]
where the time goes in v4:
time: 71.8 us; the launch traced here: 70.6 us
  Pallas kernels  69.3 us (97%)
  between operations  1.29 us (2%)
    pallas_call x1, Pallas kernels, per_device(): pl.pallas_call(functools.partial(kernel, nz, ny, nj), out_shape=(jax.Shap...  67.7 us
    pallas_call x1, Pallas kernels, per_device(): pl.pallas_call(write_out, out_shape=[jax.ShapeDtypeStruct(r.shape, F32) f...  1.56 us

profile of v4, /device:TPU:1, one launch (start us, length us, event | category | flops | bytes accessed | tf_op | source)
XLA Modules:
  0.0 70.6 jit_solution(1547123041439060990)
XLA Ops:
  1.3 67.7 %delta_step.1 = (f32[128,128]{1,0:T(8,128)}, f32[32,128]{1,0:T(8,128)}, f32[32,128]{1,0:T(8,128)}, f32[32,128]{1,0:T(8,128)}, f32[1,32]{1,0:T(1,128)}) custom-call(bf16[128,256]{1,0:T(8,128)(2,1)} %x_ref.1, bf16[32,128]{1,0:T(8,128)(2,1)} %wq_ref.1, bf16[32,128]{1,0:T(8,128)(2,1)} %wk_ref.1, bf16[32,128]{1,0:T(8,128)(2,1)} %wv_ref.1, bf16[1,32]{1,0:T(2,128)(2,1)} %bitcast.2, ...), custom_call_target="tpu_custom_call" | custom-call | tf_op jit(solution)/shard_map/delta_step/pallas_call | solution.py:601
  69.0 1.6 %write_out.1 = (f32[128,128]{1,0:T(8,128)}, f32[32,128]{1,0:T(8,128)}, f32[32,128]{1,0:T(8,128)}, f32[32,128]{1,0:T(8,128)}, f32[1,32]{1,0:T(1,128)}) custom-call(f32[128,128]{1,0:T(8,128)} %get-tuple-element.15.o_in, f32[32,128]{1,0:T(8,128)} %get-tuple-element.16.gq_in, f32[32,128]{1,0:T(8,128)} %get-tuple-element.17.gk_in, ...), custom_call_target="tpu_custom_call" | custom-call | tf_op jit(solution)/shard_map/write_out/pallas_call | solution.py:618
